TPU v7x, 256 devices: a whole 4x4x8 slice. The times are simulated.
256 devices in a mesh: ctx: 32 (over z, x), tp: 4 (over y), dp: 2 (over core).
Axes of the slice: x: 4, y: 4, z: 8, core: 2. Of those that a mesh axis runs over, the one named last changes fastest.
Arguments:
- queries: bfloat16 [16384, 4096], P(('dp', 'ctx'), 'tp'), parts along dimension 0, may hold values from -12 to 12
- keys: bfloat16 [16384, 512], P(('dp', 'ctx'), 'tp'), parts along dimension 0, may hold values from -6 to 6
- values: bfloat16 [16384, 512], P(('dp', 'ctx'), 'tp'), parts along dimension 0, may hold values from -6 to 6
- out_weight: bfloat16 [4096, 4096], P('tp'), may hold values from -0.75 to 0.75
- doc_ids: int32 [16384], P(('dp', 'ctx')), parts along dimension 0, may hold values from 0 to 8191, as said below
Outputs:
- projected: bfloat16 [16384, 4096], P(('dp', 'ctx'), 'tp'), parts along dimension 0
There are 2 independent parts, one for each index of `dp`. A program takes and returns all parts, laid end to end along the dimension named above; an argument that names none is the same for every part. Nothing has to cross between parts.
Inputs may be any that keep to these rules, and one draw needn't show every extreme that they name: `doc_ids`: ids never fall along the sequence; a document's id is the position of its first token; a document holds at most 4096 tokens, the second document holds exactly 4096, and the last token is a document of its own.
All inputs are finite; a program needn't handle non-finite values.
Results may differ from a plain program's by a relative error of at most 0.014.
Values may be sent and summed in bfloat16 or wider, within the bound.
A program may use at most 128 MiB of HBM per device.

v0:
```python
import functools
import math

import jax
import jax.numpy as jnp
from jax import lax
from jax.experimental import pallas as pl
from jax.experimental.pallas import tpu as pltpu
from jax.sharding import PartitionSpec as P

MESH = pl.DeviceIdType.MESH
TOK = 256
HEADS = 8
HD = 128
NX = 4
NZ = 8
ROW = NX * TOK
OUT = 4096
MINE = 1024
HALF = MINE // 2
CHUNKS = 2
CR = TOK // CHUNKS
LOG2E_SCALE = math.log2(math.e) / math.sqrt(HD)
NEG = -1e30
K, V = 0, 1


def kernel(
    q_hbm, k_hbm, v_hbm, w_hbm, d_ref, out_ref,
    qv, kst, kt, vb, kx, vx, dB, acc, mrow, att, wv,
    snd_a, rcv_a, snd_n, rcv_n,
    lsem, wsem, gs, gr, ds, dr,
):
    ctx = lax.axis_index("ctx")
    y = lax.axis_index("tp")
    z, x = ctx // NX, ctx % NX
    xp, xm, xo = (x + 1) % NX, (x + NX - 1) % NX, (x + 2) % NX
    dev_xp, dev_xm, dev_xo = z * NX + xp, z * NX + xm, z * NX + xo
    dev_zp = ((z + 1) % NZ) * NX + x
    dev_zm = ((z + NZ - 1) % NZ) * NX + x
    yp, ym, yo = (y + 1) % 4, (y + 3) % 4, (y + 2) % 4

    kcp = pltpu.make_async_copy(k_hbm, kst, lsem.at[0])
    vcp = pltpu.make_async_copy(v_hbm, vb.at[0, x], lsem.at[1])
    kcp.start()
    vcp.start()
    barrier = pltpu.get_barrier_semaphore()
    for dev in (dev_xp, dev_xm, dev_xo, dev_zp, dev_zm):
        pl.semaphore_signal(barrier, inc=1, device_id={"ctx": dev}, device_id_type=MESH)
    for dev in (yp, ym):
        pl.semaphore_signal(barrier, inc=1, device_id={"tp": dev}, device_id_type=MESH)
    qcp = []
    for h in range(HEADS):
        cp = pltpu.make_async_copy(q_hbm.at[:, pl.ds(h * HD, HD)], qv.at[h], lsem.at[2 + h])
        cp.start()
        qcp.append(cp)
    wcp = []
    for i in range(4):
        cp = pltpu.make_async_copy(w_hbm.at[pl.ds(i * 256, 256)], wv.at[pl.ds(i * 256, 256)], wsem.at[i])
        cp.start()
        wcp.append(cp)
    dB[...] = jnp.broadcast_to(d_ref[...], (128, TOK)).T
    acc[...] = jnp.zeros_like(acc)
    mrow[...] = jnp.full_like(mrow, NEG)
    kcp.wait()
    kt[0, x] = kst[...].T
    vcp.wait()
    pl.semaphore_wait(barrier, 7)

    pending = []

    def buf(row, col, what):
        if row == 4:
            return (kx, vx)[what]
        return (kt, vb)[what].at[row, col]

    def send(row, col, to_row, dev, whats=(K, V), when=None):
        for what in whats:
            sem = gs.at[len(pending)]
            cp = pltpu.make_async_remote_copy(
                src_ref=buf(row, col, what),
                dst_ref=buf(to_row, col, what),
                send_sem=sem,
                recv_sem=gr.at[to_row, 0 if to_row == 4 else col, what],
                device_id={"ctx": dev},
                device_id_type=MESH,
            )
            pending.append((cp, when))
            if when is None:
                cp.start()
            else:
                pl.when(when)(cp.start)

    def await_block(row, col, whats=(K, V), when=None):
        for what in whats:
            ref = buf(row, col, what)
            cp = pltpu.make_async_copy(ref, ref, gr.at[row, 0 if row == 4 else col, what])
            if when is None:
                cp.wait()
            else:
                pl.when(when)(cp.wait)

    send(0, x, 1, dev_zp)
    send(0, x, 0, dev_xp, when=x < 3)
    send(0, x, 0, dev_xm, when=x == 0)
    send(0, x, 0, dev_xo, whats=(V,), when=x == 1)
    mid = (x == 1) | (x == 2)
    await_block(0, xm, whats=(K,), when=mid)
    send(0, xm, 0, dev_xp, whats=(K,), when=mid)
    await_block(0, xp, whats=(V,), when=x == 3)
    send(0, xp, 0, dev_xm, whats=(V,), when=x == 3)

    def take_column(row):
        await_block(row, x)
        send(row, x, row + 1, dev_zp)
        send(row, x, row, dev_xp)
        send(row, x, row, dev_xm)

    def plane_step(row, lo, hi):
        kcat = jnp.concatenate([kt[row, c] for c in range(NX)], axis=1)
        vcat = vb[row].reshape(ROW, HD)
        vext = jnp.concatenate([vcat, jnp.ones_like(vcat)], axis=1)
        kpos = lax.broadcasted_iota(jnp.int32, (TOK, ROW), 1) + (z - row) * ROW
        allowed = kpos >= jnp.concatenate([dB[...]] * (ROW // 128), axis=1)

        def head(h, carry):
            update(h, slice(None), kcat, vext, allowed)
            return carry

        lax.fori_loop(lo, hi, head, 0)

    def update(h, rows, kcat, vext, allowed):
        s = jnp.dot(qv[h, rows], kcat, preferred_element_type=jnp.float32)
        s = jnp.where(allowed, s, NEG)
        old = mrow[h, rows]
        new = jnp.maximum(old, jnp.max(s, axis=1, keepdims=True))
        p = jnp.exp2((s - jnp.concatenate([new] * (s.shape[1] // 128), axis=1)) * LOG2E_SCALE)
        factor = jnp.exp2((old - new) * LOG2E_SCALE)
        acc[h, rows] = acc[h, rows] * jnp.concatenate([factor, factor], axis=1) + jnp.dot(
            p.astype(jnp.bfloat16), vext, preferred_element_type=jnp.float32
        )
        mrow[h, rows] = new

    take_column(1)
    await_block(1, xm)
    send(1, xm, 1, dev_xp)
    for cp in qcp:
        cp.wait()
    take_column(2)
    await_block(1, xp)
    await_block(1, xo)
    send(1, xo, 2, dev_zp)
    plane_step(1, 0, 4)
    take_column(3)
    plane_step(1, 4, 8)
    await_block(2, xo)
    send(2, xo, 3, dev_zp)
    await_block(2, xp)
    await_block(2, xm)
    plane_step(2, 0, 4)
    await_block(4, x)

    def send4(dev, whats, when):
        for what in whats:
            cp = pltpu.make_async_remote_copy(
                src_ref=buf(4, x, what),
                dst_ref=buf(0, x, what),
                send_sem=gs.at[len(pending)],
                recv_sem=gr.at[0, x, what],
                device_id={"ctx": dev},
                device_id_type=MESH,
            )
            pending.append((cp, when))
            pl.when(when)(cp.start)

    send4(dev_xm, (K, V), x > 0)
    send4(dev_xp, (K, V), x == 3)
    send4(dev_xo, (K,), x == 2)
    plane_step(2, 4, 8)
    await_block(3, xp)
    await_block(3, xm)
    await_block(3, xo)
    await_block(0, xp, whats=(V,), when=mid)
    send(0, xp, 0, dev_xm, whats=(V,), when=mid)
    await_block(0, xm, whats=(K,), when=x == 0)
    send(0, xm, 0, dev_xp, whats=(K,), when=x == 0)
    plane_step(3, 0, 8)

    await_block(0, xm, whats=(K,), when=x == 3)
    await_block(0, xm, whats=(V,))
    await_block(0, xp, whats=(K,))
    await_block(0, xp, whats=(V,), when=x == 0)
    await_block(0, xo)
    for cp in wcp:
        cp.wait()

    def rs_copy(c, slot, src, dst, dev):
        return pltpu.make_async_remote_copy(
            src_ref=src,
            dst_ref=dst,
            send_sem=ds.at[c, slot],
            recv_sem=dr.at[c, slot],
            device_id={"tp": dev},
            device_id_type=MESH,
        )

    def copies(c):
        return (
            rs_copy(c, 0, snd_a.at[c, 0], rcv_a.at[c, 0], yp),
            rs_copy(c, 1, snd_a.at[c, 1], rcv_a.at[c, 1], ym),
            rs_copy(c, 2, snd_n.at[c, 0], rcv_n.at[c, 0], yp),
            rs_copy(c, 3, snd_n.at[c, 1], rcv_n.at[c, 1], ym),
            rs_copy(c, 4, snd_n.at[c, 2], rcv_n.at[c, 2], yp),
            rs_copy(c, 5, snd_n.at[c, 3], rcv_n.at[c, 3], ym),
        )

    def project(c, dest, half):
        cols = pl.ds(pl.multiple_of(dest * MINE + half * HALF, HALF), HALF)
        return jnp.dot(att[c], wv[:, cols], preferred_element_type=jnp.float32)

    lane = lax.broadcasted_iota(jnp.int32, (CR, ROW), 1)
    own_pos = lane + z * ROW - jnp.where(lane // TOK > x, 4 * ROW, 0)
    ext_lane = lax.broadcasted_iota(jnp.int32, (CR, TOK), 1)
    last_pos = jnp.concatenate([own_pos, ext_lane + ((z - 4) * ROW + x * TOK)], axis=1)
    row_at = lax.broadcasted_iota(jnp.int32, (CR, ROW + TOK), 0) + ctx * TOK

    def finish(c, carry):
        rows = pl.ds(pl.multiple_of(c * CR, CR), CR)
        kcat = jnp.concatenate([kt[0, i] for i in range(NX)] + [kx[...]], axis=1)
        vcat = jnp.concatenate([vb[0].reshape(ROW, HD), vx[...]], axis=0)
        vext = jnp.concatenate([vcat, jnp.ones_like(vcat)], axis=1)
        first = jnp.concatenate([dB[rows]] * ((ROW + TOK) // 128), axis=1)
        allowed = (last_pos >= first) & (last_pos <= row_at + c * CR)

        def head(h, carry):
            update(h, rows, kcat, vext, allowed)
            a = acc[h, rows]
            att[c, :, pl.ds(pl.multiple_of(h * HD, HD), HD)] = (a[:, :HD] / a[:, HD:]).astype(jnp.bfloat16)
            return carry

        lax.fori_loop(0, HEADS, head, 0)
        cps = copies(c)
        for i, (dest, half, buffer, slot) in enumerate(
            ((yo, 0, snd_a, 0), (yo, 1, snd_a, 1), (yp, 1, snd_n, 0), (ym, 0, snd_n, 1))
        ):
            buffer[c, slot] = project(c, dest, half).astype(jnp.bfloat16)
            cps[i].start()
        return carry

    lax.fori_loop(0, CHUNKS, finish, 0)

    def relay(c, carry):
        cps = copies(c)
        for i, (dest, half) in enumerate(((yp, 0), (ym, 1))):
            part = project(c, dest, half)
            cps[i].wait_recv()
            snd_n[c, 2 + i] = (part + rcv_a[c, i].astype(jnp.float32)).astype(jnp.bfloat16)
            cps[4 + i].start()
        return carry

    lax.fori_loop(0, CHUNKS, relay, 0)

    def collect(c, carry):
        rows = pl.ds(pl.multiple_of(c * CR, CR), CR)
        cps = copies(c)
        own = [project(c, y, half) for half in (0, 1)]
        for i in range(2, 6):
            cps[i].wait_recv()
        out_ref[rows, :HALF] = (
            own[0] + rcv_n[c, 2].astype(jnp.float32) + rcv_n[c, 1].astype(jnp.float32)
        ).astype(jnp.bfloat16)
        out_ref[rows, HALF:] = (
            own[1] + rcv_n[c, 0].astype(jnp.float32) + rcv_n[c, 3].astype(jnp.float32)
        ).astype(jnp.bfloat16)
        for cp in cps:
            cp.wait_send()
        return carry

    lax.fori_loop(0, CHUNKS, collect, 0)
    for cp, when in pending:
        if when is None:
            cp.wait_send()
        else:
            pl.when(when)(cp.wait_send)


def body(queries, keys, values, out_weight, doc_ids):
    bf, f32 = jnp.bfloat16, jnp.float32
    any_spec = pl.BlockSpec(memory_space=pl.ANY)
    vmem = pl.BlockSpec(memory_space=pltpu.VMEM)
    return pl.pallas_call(
        kernel,
        out_shape=jax.ShapeDtypeStruct((TOK, MINE), bf),
        in_specs=[any_spec] * 4 + [vmem],
        out_specs=vmem,
        scratch_shapes=[
            pltpu.VMEM((HEADS, TOK, HD), bf),
            pltpu.VMEM((TOK, HD), bf),
            pltpu.VMEM((4, NX, HD, TOK), bf),
            pltpu.VMEM((4, NX, TOK, HD), bf),
            pltpu.VMEM((HD, TOK), bf),
            pltpu.VMEM((TOK, HD), bf),
            pltpu.VMEM((TOK, 128), jnp.int32),
            pltpu.VMEM((HEADS, TOK, 2 * HD), f32),
            pltpu.VMEM((HEADS, TOK, 128), f32),
            pltpu.VMEM((CHUNKS, CR, HEADS * HD), bf),
            pltpu.VMEM((HEADS * HD, OUT), bf),
            pltpu.VMEM((CHUNKS, 2, CR, HALF), bf),
            pltpu.VMEM((CHUNKS, 2, CR, HALF), bf),
            pltpu.VMEM((CHUNKS, 4, CR, HALF), bf),
            pltpu.VMEM((CHUNKS, 4, CR, HALF), bf),
            pltpu.SemaphoreType.DMA((2 + HEADS,)),
            pltpu.SemaphoreType.DMA((4,)),
            pltpu.SemaphoreType.DMA((64,)),
            pltpu.SemaphoreType.DMA((5, NX, 2)),
            pltpu.SemaphoreType.DMA((CHUNKS, 6)),
            pltpu.SemaphoreType.DMA((CHUNKS, 6)),
        ],
        compiler_params=pltpu.CompilerParams(
            collective_id=0, has_side_effects=True, vmem_limit_bytes=48 << 20
        ),
        cost_estimate=pl.CostEstimate(flops=7 * 10**9, bytes_accessed=10**7, transcendentals=9 * 10**6),
    )(queries, keys, values, out_weight, doc_ids.reshape(1, TOK))


def solution(mesh):
    placed = (
        P(("dp", "ctx"), "tp"),
        P(("dp", "ctx"), "tp"),
        P(("dp", "ctx"), "tp"),
        P("tp", None),
        P(("dp", "ctx")),
    )
    return jax.shard_map(
        body, mesh=mesh, in_specs=placed, out_specs=P(("dp", "ctx"), "tp"), check_vma=False
    )
```

profile of v0, /device:TPU:24, one launch (start us, length us, event | category | flops | bytes accessed | tf_op | source)
XLA Modules:
  0.0 70.7 jit_solution(32369707570750923)
XLA Ops:
  0.0 0.0 copy-start
  0.0 1.0 %copy-done = bf16[256,1024]{1,0:T(8,128)(2,1)S(1)} copy-done((bf16[256,1024]{1,0:T(8,128)(2,1)S(1)}, bf16[256,1024]{1,0:T(8,128)(2,1)}, u32[]{:S(2)}) %copy-start) | copy-done | bytes 524312
  1.0 0.0 copy-start.1
  1.0 0.8 %copy-done.1 = bf16[256,128]{1,0:T(8,128)(2,1)S(1)} copy-done((bf16[256,128]{1,0:T(8,128)(2,1)S(1)}, bf16[256,128]{1,0:T(8,128)(2,1)}, u32[]{:S(2)}) %copy-start.1) | copy-done | bytes 65560
  1.9 0.0 copy-start.2
  1.9 0.8 %copy-done.2 = bf16[256,128]{1,0:T(8,128)(2,1)S(1)} copy-done((bf16[256,128]{1,0:T(8,128)(2,1)S(1)}, bf16[256,128]{1,0:T(8,128)(2,1)}, u32[]{:S(2)}) %copy-start.2) | copy-done | bytes 65560
  2.7 0.0 copy-start.3
  2.7 0.7 copy-done.3
  3.4 66.5 %shard_map.55 = bf16[256,1024]{1,0:T(8,128)(2,1)S(1)} custom-call(bf16[256,1024]{1,0:T(8,128)(2,1)S(1)} %copy-done, bf16[256,128]{1,0:T(8,128)(2,1)S(1)} %copy-done.1, bf16[256,128]{1,0:T(8,128)(2,1)S(1)} %copy-done.2, bf16[1024,4096]{1,0:T(8,128)(2,1)} %w_hbm.1, s32[1,256]{1,0:T(1,128)S(1)} %bitcast.1), custom_call_target="tpu_custom_call" | custom-call | flops 7000000000 | bytes 10000000 | tf_op jit(solution)/shard_map/pallas_call | solution.py:291
  69.9 0.8 %copy.7 = bf16[256,1024]{1,0:T(8,128)(2,1)} copy(bf16[256,1024]{1,0:T(8,128)(2,1)S(1)} %shard_map.55) | data formatting | bytes 1048576
Async XLA Ops:
  0.0 1.0 %copy-start = (bf16[256,1024]{1,0:T(8,128)(2,1)S(1)}, bf16[256,1024]{1,0:T(8,128)(2,1)}, u32[]{:S(2)}) copy-start(bf16[256,1024]{1,0:T(8,128)(2,1)} %q_hbm.1) | copy-start | bytes 1572868
  1.0 0.8 %copy-start.1 = (bf16[256,128]{1,0:T(8,128)(2,1)S(1)}, bf16[256,128]{1,0:T(8,128)(2,1)}, u32[]{:S(2)}) copy-start(bf16[256,128]{1,0:T(8,128)(2,1)} %k_hbm.1) | copy-start | bytes 196612
  1.9 0.8 %copy-start.2 = (bf16[256,128]{1,0:T(8,128)(2,1)S(1)}, bf16[256,128]{1,0:T(8,128)(2,1)}, u32[]{:S(2)}) copy-start(bf16[256,128]{1,0:T(8,128)(2,1)} %v_hbm.1) | copy-start | bytes 196612
  2.7 0.7 copy-start.3
where the time goes:
time: 71.4 us; the launch traced here: 70.7 us
  Pallas kernels  66.5 us (93%)
  local copies, waits for them, and re-layouts  4.19 us (6%)
    pallas_call x1, Pallas kernels, body(): pl.pallas_call(kernel, out_shape=jax.ShapeDtypeStruct((TOK, MINE), bf), i...  66.5 us
    unnamed x9, local copies, waits for them, and re-layouts  4.19 us

commit v1 on v0

v1 whole, which is shorter than its diff:
```python
import math

import jax
import jax.numpy as jnp
from jax import lax
from jax.experimental import pallas as pl
from jax.experimental.pallas import tpu as pltpu
from jax.sharding import PartitionSpec as P

MESH = pl.DeviceIdType.MESH
TOK = 256
HEADS = 8
HD = 128
NX = 4
NZ = 8
ROW = NX * TOK
OUT = 4096
MINE = 1024
HALF = MINE // 2
CHUNKS = 2
CR = TOK // CHUNKS
GROUPS = HEADS
PER = GROUPS // CHUNKS
LANES = 2 * CR
ONES = 16
LOG2E_SCALE = math.log2(math.e) / math.sqrt(HD)
NEG = -1e30
K, V = 0, 1
BOTH = ((K,), (V,))


def kernel(
    q_hbm, k_hbm, v_hbm, w_hbm, d_ref, out_ref,
    qst, vst, qt, kb, vt, kx, vx, tk, tv, ok, ov, d2, acc, top, sa, sb, att, wv,
    snd_a, rcv_a, snd_n, rcv_n,
    lsem, wsem, gs, gr, tr, osem, ds, dr,
):
    ctx = lax.axis_index("ctx")
    y = lax.axis_index("tp")
    z, x = ctx // NX, ctx % NX
    xp, xm, xo = (x + 1) % NX, (x + NX - 1) % NX, (x + 2) % NX
    dev_xp, dev_xm, dev_xo = z * NX + xp, z * NX + xm, z * NX + xo

    def plane(dz):
        return ((z + dz + NZ) % NZ) * NX + x

    dev_zp = plane(1)
    yp, ym, yo = (y + 1) % 4, (y + 3) % 4, (y + 2) % 4

    kcp = pltpu.make_async_copy(k_hbm, kb.at[0, x], lsem.at[0])
    vcp = pltpu.make_async_copy(v_hbm, vst, lsem.at[1])
    kcp.start()
    vcp.start()
    barrier = pltpu.get_barrier_semaphore()
    for dev in (dev_xp, dev_xm, dev_xo, plane(1), plane(-1), plane(2), plane(-2)):
        pl.semaphore_signal(barrier, inc=1, device_id={"ctx": dev}, device_id_type=MESH)
    for dev in (yp, ym):
        pl.semaphore_signal(barrier, inc=1, device_id={"tp": dev}, device_id_type=MESH)
    qcp = pltpu.make_async_copy(q_hbm, qst, lsem.at[2])
    qcp.start()
    wcp = []
    for i in range(4):
        cp = pltpu.make_async_copy(w_hbm.at[pl.ds(i * 256, 256)], wv.at[pl.ds(i * 256, 256)], wsem.at[i])
        cp.start()
        wcp.append(cp)
    for c in range(CHUNKS):
        half = d_ref[:, c * CR : (c + 1) * CR]
        d2[c] = jnp.concatenate([half, half], axis=1)
    acc[...] = jnp.zeros_like(acc)
    top[...] = jnp.full_like(top, NEG)
    vcp.wait()
    vt[0, x] = vst[...].T
    kcp.wait()
    qcp.wait()
    for c in range(CHUNKS):
        for h in range(HEADS):
            part = qst[c * CR : (c + 1) * CR, h * HD : (h + 1) * HD].T
            qt[c * PER + h // 2, :, (h % 2) * CR : (h % 2 + 1) * CR] = part
    pl.semaphore_wait(barrier, 9)

    pending = []

    def buf(row, col, what):
        if row == 4:
            return (kx, vx)[what]
        if row == 5:
            return (tk, tv)[what]
        if row == 6:
            return (ok, ov)[what]
        return (kb, vt)[what].at[row, col]

    def arrival(row, col, what):
        if row == 5:
            return tr.at[what]
        if row == 6:
            return osem.at[what]
        return gr.at[row, 0 if row == 4 else col, what]

    def send(src, dst, dev, whats=(K, V), when=None):
        for what in whats:
            cp = pltpu.make_async_remote_copy(
                src_ref=buf(*src, what),
                dst_ref=buf(*dst, what),
                send_sem=gs.at[len(pending)],
                recv_sem=arrival(*dst, what),
                device_id={"ctx": dev},
                device_id_type=MESH,
            )
            pending.append((cp, when))
            if when is None:
                cp.start()
            else:
                pl.when(when)(cp.start)

    def take(row, col, whats=(K, V), when=None):
        for what in whats:
            ref = buf(row, col, what)
            cp = pltpu.make_async_copy(ref, ref, arrival(row, col, what))
            if when is None:
                cp.wait()
            else:
                pl.when(when)(cp.wait)

    for w in BOTH:
        send((0, x), (1, x), dev_zp, w)
        send((0, x), (0, x), dev_xp, w, x < 3)
        send((0, x), (0, x), dev_xo, w, x < 2)
        send((0, x), (6, x), dev_xo, w, x >= 2)
        send((0, x), (5, x), plane(-2), w)
        send((0, x), (0, x), dev_xm, w, x == 0)

    def sides(row, w):
        send((row, x), (row, x), dev_xp, w)
        send((row, x), (row, x), dev_xm, w)

    key_row = lax.broadcasted_iota(jnp.int32, (TOK, LANES), 0)

    def sweep(blocks, lo, hi, causal=False):
        tiles = [blocks[i : i + 2] for i in range(0, len(blocks), 2)]

        def scores(g, dst, causal):
            first = d2[g // PER]
            high = None
            for j, tile in enumerate(tiles):
                s = jnp.dot(
                    jnp.concatenate([b[0][...] for b in tile], axis=0), qt[g],
                    preferred_element_type=jnp.float32,
                )
                pos = jnp.concatenate([key_row + b[2] for b in tile], axis=0)
                allowed = pos >= first
                if causal and j == 0:
                    lane = lax.broadcasted_iota(jnp.int32, (1, LANES), 1)
                    at = ctx * TOK + (g // PER) * CR + lane % CR
                    allowed = allowed & (pos <= at)
                s = jnp.where(allowed, s, NEG)
                dst[j, : s.shape[0]] = s
                part = jnp.max(s.reshape(s.shape[0] // 8, 8, LANES), axis=0)
                high = part if high is None else jnp.maximum(high, part)
            return high

        def absorb(g, src, high, nxt):
            old = top[g]
            new = jnp.maximum(old, jnp.max(high, axis=0, keepdims=True))
            top[g] = new
            factor = jnp.exp2((old - new) * LOG2E_SCALE)
            after = scores(jnp.minimum(g + 1, hi - 1), nxt, causal)
            total = None
            for j, tile in enumerate(tiles):
                n = len(tile) * TOK
                p = jnp.exp2((src[j, :n] - new) * LOG2E_SCALE).astype(jnp.bfloat16)
                values = jnp.concatenate([b[1][...] for b in tile], axis=1)
                values = jnp.concatenate([values, jnp.ones((ONES, n), jnp.bfloat16)], axis=0)
                part = jnp.dot(values, p, preferred_element_type=jnp.float32)
                total = part if total is None else total + part
            acc[g] = acc[g] * factor + total
            return after

        def two(t, high):
            g = lo + 2 * t
            high = absorb(g, sa, high, sb)
            return absorb(g + 1, sb, high, sa)

        lax.fori_loop(0, (hi - lo) // 2, two, scores(lo, sa, causal))

    def block(row, col, first):
        return (buf(row, col, K), buf(row, col, V), first)

    def far(row, col):
        return block(row, col, (z - row) * ROW + col * TOK)

    def mixed(col):
        return block(0, col, (z - jnp.where(col < x, 0, 4)) * ROW + col * TOK)

    for w in BOTH:
        take(1, x, w)
        send((1, x), (2, x), dev_zp, w)
        sides(1, w)
    for w in BOTH:
        take(5, x, w)
        send((5, x), (4, x), plane(-2), w)
    for w in BOTH:
        take(6, x, w, x < 2)
        send((6, x), (1, xo), dev_zp, w, x < 2)
        take(0, xo, w, x >= 2)
        send((0, xo), (1, xo), dev_zp, w, x >= 2)
    for w in BOTH:
        take(2, x, w)
        send((2, x), (3, x), dev_zp, w)
        sides(2, w)
    take(1, xp)
    take(1, xm)
    sweep([block(0, x, ctx * TOK), far(1, x), far(1, xp), far(1, xm)], 0, GROUPS, causal=True)
    for w in BOTH:
        take(1, xo, w)
        send((1, xo), (2, xo), dev_zp, w)
    for w in BOTH:
        take(4, x, w)
        send((4, x), (0, x), dev_xm, w, x > 0)
        send((4, x), (0, x), dev_xo, w, x > 1)
        send((4, x), (0, x), dev_xp, w, x == 3)
    for w in BOTH:
        take(3, x, w)
        sides(3, w)
    take(2, xp)
    take(2, xm)
    sweep([far(1, xo), far(2, x), far(2, xp), far(2, xm)], 0, GROUPS)
    for w in BOTH:
        take(2, xo, w)
        send((2, xo), (3, xo), dev_zp, w)
    take(0, xp)
    take(0, xm)
    sweep([far(2, xo), mixed(xp), mixed(xm), block(4, x, (z - 4) * ROW + x * TOK)], 0, GROUPS)
    take(3, xp)
    take(3, xm)
    take(0, xo, when=x < 2)
    for cp in wcp:
        cp.wait()

    def rs_copy(c, slot, src, dst, dev):
        return pltpu.make_async_remote_copy(
            src_ref=src,
            dst_ref=dst,
            send_sem=ds.at[c, slot],
            recv_sem=dr.at[c, slot],
            device_id={"tp": dev},
            device_id_type=MESH,
        )

    def copies(c):
        return (
            rs_copy(c, 0, snd_a.at[c, 0], rcv_a.at[c, 0], yp),
            rs_copy(c, 1, snd_a.at[c, 1], rcv_a.at[c, 1], ym),
            rs_copy(c, 2, snd_n.at[c, 0], rcv_n.at[c, 0], yp),
            rs_copy(c, 3, snd_n.at[c, 1], rcv_n.at[c, 1], ym),
            rs_copy(c, 4, snd_n.at[c, 2], rcv_n.at[c, 2], yp),
            rs_copy(c, 5, snd_n.at[c, 3], rcv_n.at[c, 3], ym),
        )

    def project(c, dest, half):
        cols = pl.ds(pl.multiple_of(dest * MINE + half * HALF, HALF), HALF)
        return jnp.dot(att[c], wv[:, cols], preferred_element_type=jnp.float32)

    def finish(c):
        sweep([far(3, x), far(3, xp), far(3, xm), mixed(xo)], c * PER, (c + 1) * PER)
        if c == 0:
            take(3, xo)
        sweep([far(3, xo)], c * PER, (c + 1) * PER)
        for i in range(PER):
            a = acc[c * PER + i]
            o = a[:HD] / a[HD : HD + 1]
            for side in range(2):
                h = 2 * i + side
                att[c, :, h * HD : (h + 1) * HD] = o[:, side * CR : (side + 1) * CR].T.astype(jnp.bfloat16)
        cps = copies(c)
        for i, (dest, half, buffer, slot) in enumerate(
            ((yo, 0, snd_a, 0), (yo, 1, snd_a, 1), (yp, 1, snd_n, 0), (ym, 0, snd_n, 1))
        ):
            buffer[c, slot] = project(c, dest, half).astype(jnp.bfloat16)
            cps[i].start()

    def relay(c):
        cps = copies(c)
        for i, (dest, half) in enumerate(((yp, 0), (ym, 1))):
            part = project(c, dest, half)
            cps[i].wait_recv()
            snd_n[c, 2 + i] = (part + rcv_a[c, i].astype(jnp.float32)).astype(jnp.bfloat16)
            cps[4 + i].start()

    def collect(c):
        cps = copies(c)
        own = [project(c, y, half) for half in (0, 1)]
        for i in range(2, 6):
            cps[i].wait_recv()
        rows = slice(c * CR, (c + 1) * CR)
        out_ref[rows, :HALF] = (
            own[0] + rcv_n[c, 2].astype(jnp.float32) + rcv_n[c, 1].astype(jnp.float32)
        ).astype(jnp.bfloat16)
        out_ref[rows, HALF:] = (
            own[1] + rcv_n[c, 0].astype(jnp.float32) + rcv_n[c, 3].astype(jnp.float32)
        ).astype(jnp.bfloat16)

    finish(0)
    finish(1)
    relay(0)
    relay(1)
    collect(0)
    collect(1)
    for c in range(CHUNKS):
        for cp in copies(c):
            cp.wait_send()
    for cp, when in pending:
        if when is None:
            cp.wait_send()
        else:
            pl.when(when)(cp.wait_send)


def body(queries, keys, values, out_weight, doc_ids):
    bf, f32 = jnp.bfloat16, jnp.float32
    hbm = pl.BlockSpec(memory_space=pltpu.HBM)
    vmem = pl.BlockSpec(memory_space=pltpu.VMEM)
    dma = pltpu.SemaphoreType.DMA
    return pl.pallas_call(
        kernel,
        out_shape=jax.ShapeDtypeStruct((TOK, MINE), bf),
        in_specs=[hbm] * 4 + [vmem],
        out_specs=vmem,
        scratch_shapes=[
            pltpu.VMEM((TOK, HEADS * HD), bf),
            pltpu.VMEM((TOK, HD), bf),
            pltpu.VMEM((GROUPS, HD, LANES), bf),
            pltpu.VMEM((4, NX, TOK, HD), bf),
            pltpu.VMEM((4, NX, HD, TOK), bf),
            pltpu.VMEM((TOK, HD), bf),
            pltpu.VMEM((HD, TOK), bf),
            pltpu.VMEM((TOK, HD), bf),
            pltpu.VMEM((HD, TOK), bf),
            pltpu.VMEM((TOK, HD), bf),
            pltpu.VMEM((HD, TOK), bf),
            pltpu.VMEM((CHUNKS, 1, LANES), jnp.int32),
            pltpu.VMEM((GROUPS, HD + ONES, LANES), f32),
            pltpu.VMEM((GROUPS, 1, LANES), f32),
            pltpu.VMEM((2, 2 * TOK, LANES), f32),
            pltpu.VMEM((2, 2 * TOK, LANES), f32),
            pltpu.VMEM((CHUNKS, CR, HEADS * HD), bf),
            pltpu.VMEM((HEADS * HD, OUT), bf),
            pltpu.VMEM((CHUNKS, 2, CR, HALF), bf),
            pltpu.VMEM((CHUNKS, 2, CR, HALF), bf),
            pltpu.VMEM((CHUNKS, 4, CR, HALF), bf),
            pltpu.VMEM((CHUNKS, 4, CR, HALF), bf),
            dma((3,)),
            dma((4,)),
            dma((64,)),
            dma((5, NX, 2)),
            dma((2,)),
            dma((2,)),
            dma((CHUNKS, 6)),
            dma((CHUNKS, 6)),
        ],
        compiler_params=pltpu.CompilerParams(
            collective_id=0, has_side_effects=True, vmem_limit_bytes=60 << 20
        ),
        cost_estimate=pl.CostEstimate(flops=7 * 10**9, bytes_accessed=10**7, transcendentals=9 * 10**6),
    )(queries, keys, values, out_weight, doc_ids.reshape(1, TOK))


def solution(mesh):
    placed = (
        P(("dp", "ctx"), "tp"),
        P(("dp", "ctx"), "tp"),
        P(("dp", "ctx"), "tp"),
        P("tp", None),
        P(("dp", "ctx")),
    )
    return jax.shard_map(
        body, mesh=mesh, in_specs=placed, out_specs=P(("dp", "ctx"), "tp"), check_vma=False
    )
```

time: 71.4 us -> 59.9 us (0.84)
  the two profiles are of different devices: /device:TPU:24 before, /device:TPU:1 now
where the time goes in v1:
time: 59.9 us; the launch traced here: 59.8 us
  Pallas kernels  57.9 us (97%)
  local copies, waits for them, and re-layouts  1.87 us (3%)
    pallas_call x1, Pallas kernels, body(): pl.pallas_call(kernel, out_shape=jax.ShapeDtypeStruct((TOK, MINE), bf), i...  57.9 us
    unnamed x1, local copies, waits for them, and re-layouts  1.87 us

profile of v1, /device:TPU:1, one launch (start us, length us, event | category | flops | bytes accessed | tf_op | source)
XLA Modules:
  0.0 59.8 jit_solution(2107610607290615772)
XLA Ops:
  0.0 57.9 %shard_map.55 = bf16[256,1024]{1,0:T(8,128)(2,1)} custom-call(bf16[256,1024]{1,0:T(8,128)(2,1)} %q_hbm.1, bf16[256,128]{1,0:T(8,128)(2,1)} %k_hbm.1, bf16[256,128]{1,0:T(8,128)(2,1)} %v_hbm.1, bf16[1024,4096]{1,0:T(8,128)(2,1)} %w_hbm.1, s32[1,256]{1,0:T(1,128)} %bitcast.1), custom_call_target="tpu_custom_call" | custom-call | flops 7000000000 | bytes 10000000 | tf_op jit(solution)/shard_map/pallas_call | solution.py:323
  57.9 1.9 %copy.7 = bf16[256,1024]{1,0:T(8,128)(2,1)} copy(bf16[256,1024]{1,0:T(8,128)(2,1)} %shard_map.55) | data formatting | bytes 1048576

commit v2 on v1

--- a/solution.py
+++ b/solution.py
@@ -17,11 +17,12 @@
 OUT = 4096
 MINE = 1024
 HALF = MINE // 2
-CHUNKS = 2
+CHUNKS = 4
 CR = TOK // CHUNKS
-GROUPS = HEADS
-PER = GROUPS // CHUNKS
-LANES = 2 * CR
+LANES = 256
+SIDE = LANES // CR
+PER = HEADS // SIDE
+GROUPS = CHUNKS * PER
 ONES = 16
 LOG2E_SCALE = math.log2(math.e) / math.sqrt(HD)
 NEG = -1e30
@@ -58,24 +59,9 @@
         pl.semaphore_signal(barrier, inc=1, device_id={"tp": dev}, device_id_type=MESH)
     qcp = pltpu.make_async_copy(q_hbm, qst, lsem.at[2])
     qcp.start()
-    wcp = []
-    for i in range(4):
-        cp = pltpu.make_async_copy(w_hbm.at[pl.ds(i * 256, 256)], wv.at[pl.ds(i * 256, 256)], wsem.at[i])
-        cp.start()
-        wcp.append(cp)
-    for c in range(CHUNKS):
-        half = d_ref[:, c * CR : (c + 1) * CR]
-        d2[c] = jnp.concatenate([half, half], axis=1)
-    acc[...] = jnp.zeros_like(acc)
-    top[...] = jnp.full_like(top, NEG)
     vcp.wait()
     vt[0, x] = vst[...].T
     kcp.wait()
-    qcp.wait()
-    for c in range(CHUNKS):
-        for h in range(HEADS):
-            part = qst[c * CR : (c + 1) * CR, h * HD : (h + 1) * HD].T
-            qt[c * PER + h // 2, :, (h % 2) * CR : (h % 2 + 1) * CR] = part
     pl.semaphore_wait(barrier, 9)
 
     pending = []
@@ -129,13 +115,25 @@
         send((0, x), (5, x), plane(-2), w)
         send((0, x), (0, x), dev_xm, w, x == 0)
 
+    for c in range(CHUNKS):
+        d2[c] = jnp.concatenate([d_ref[:, c * CR : (c + 1) * CR]] * SIDE, axis=1)
+    acc[...] = jnp.zeros_like(acc)
+    top[...] = jnp.full_like(top, NEG)
+    qcp.wait()
+    for c in range(CHUNKS):
+        for i in range(PER):
+            heads = range(i * SIDE, (i + 1) * SIDE)
+            part = [qst[c * CR : (c + 1) * CR, h * HD : (h + 1) * HD] for h in heads]
+            qt[c * PER + i] = jnp.concatenate(part, axis=0).T
+
     def sides(row, w):
         send((row, x), (row, x), dev_xp, w)
         send((row, x), (row, x), dev_xm, w)
 
     key_row = lax.broadcasted_iota(jnp.int32, (TOK, LANES), 0)
 
-    def sweep(blocks, lo, hi, causal=False):
+    def sweep(blocks, lo, count, causal=False):
+        hi = lo + count
         tiles = [blocks[i : i + 2] for i in range(0, len(blocks), 2)]
 
         def scores(g, dst, causal):
@@ -158,12 +156,12 @@
                 high = part if high is None else jnp.maximum(high, part)
             return high
 
-        def absorb(g, src, high, nxt):
+        def absorb(g, src, high, nxt, more=True):
             old = top[g]
             new = jnp.maximum(old, jnp.max(high, axis=0, keepdims=True))
             top[g] = new
             factor = jnp.exp2((old - new) * LOG2E_SCALE)
-            after = scores(jnp.minimum(g + 1, hi - 1), nxt, causal)
+            after = scores(jnp.minimum(g + 1, hi - 1), nxt, causal) if more else None
             total = None
             for j, tile in enumerate(tiles):
                 n = len(tile) * TOK
@@ -175,12 +173,17 @@
             acc[g] = acc[g] * factor + total
             return after
 
+        high = scores(lo, sa, causal)
+        if count == 2:
+            absorb(lo + 1, sb, absorb(lo, sa, high, sb), sa, more=False)
+            return
+
         def two(t, high):
             g = lo + 2 * t
             high = absorb(g, sa, high, sb)
             return absorb(g + 1, sb, high, sa)
 
-        lax.fori_loop(0, (hi - lo) // 2, two, scores(lo, sa, causal))
+        lax.fori_loop(0, count // 2, two, high)
 
     def block(row, col, first):
         return (buf(row, col, K), buf(row, col, V), first)
@@ -195,44 +198,52 @@
         take(1, x, w)
         send((1, x), (2, x), dev_zp, w)
         sides(1, w)
-    for w in BOTH:
-        take(5, x, w)
-        send((5, x), (4, x), plane(-2), w)
     for w in BOTH:
         take(6, x, w, x < 2)
         send((6, x), (1, xo), dev_zp, w, x < 2)
         take(0, xo, w, x >= 2)
         send((0, xo), (1, xo), dev_zp, w, x >= 2)
+    wcp = []
+    for i in range(4):
+        cp = pltpu.make_async_copy(w_hbm.at[pl.ds(i * 256, 256)], wv.at[pl.ds(i * 256, 256)], wsem.at[i])
+        cp.start()
+        wcp.append(cp)
+    for w in BOTH:
+        take(5, x, w)
+        send((5, x), (4, x), plane(-2), w)
     for w in BOTH:
         take(2, x, w)
         send((2, x), (3, x), dev_zp, w)
         sides(2, w)
     take(1, xp)
     take(1, xm)
-    sweep([block(0, x, ctx * TOK), far(1, x), far(1, xp), far(1, xm)], 0, GROUPS, causal=True)
+    near = [block(0, x, ctx * TOK), far(1, x), far(1, xp), far(1, xm)]
+    sweep(near, 0, GROUPS // 2, causal=True)
     for w in BOTH:
         take(1, xo, w)
         send((1, xo), (2, xo), dev_zp, w)
     for w in BOTH:
         take(4, x, w)
+        send((4, x), (0, x), dev_xo, w, x > 1)
         send((4, x), (0, x), dev_xm, w, x > 0)
-        send((4, x), (0, x), dev_xo, w, x > 1)
         send((4, x), (0, x), dev_xp, w, x == 3)
+    sweep(near, GROUPS // 2, GROUPS // 2, causal=True)
     for w in BOTH:
         take(3, x, w)
         sides(3, w)
+    sweep([far(1, xo), far(2, x), far(3, x), block(4, x, (z - 4) * ROW + x * TOK)], 0, GROUPS)
+    for w in BOTH:
+        take(2, xo, w)
+        send((2, xo), (3, xo), dev_zp, w)
     take(2, xp)
     take(2, xm)
-    sweep([far(1, xo), far(2, x), far(2, xp), far(2, xm)], 0, GROUPS)
-    for w in BOTH:
-        take(2, xo, w)
-        send((2, xo), (3, xo), dev_zp, w)
     take(0, xp)
     take(0, xm)
-    sweep([far(2, xo), mixed(xp), mixed(xm), block(4, x, (z - 4) * ROW + x * TOK)], 0, GROUPS)
+    sweep([far(2, xp), far(2, xm), mixed(xp), mixed(xm)], 0, GROUPS)
     take(3, xp)
     take(3, xm)
     take(0, xo, when=x < 2)
+    take(3, xo)
     for cp in wcp:
         cp.wait()
 
@@ -260,54 +271,50 @@
         cols = pl.ds(pl.multiple_of(dest * MINE + half * HALF, HALF), HALF)
         return jnp.dot(att[c], wv[:, cols], preferred_element_type=jnp.float32)
 
-    def finish(c):
-        sweep([far(3, x), far(3, xp), far(3, xm), mixed(xo)], c * PER, (c + 1) * PER)
-        if c == 0:
-            take(3, xo)
-        sweep([far(3, xo)], c * PER, (c + 1) * PER)
+    def finish(c, carry):
+        sweep([far(2, xo), far(3, xp), far(3, xm), mixed(xo), far(3, xo)], c * PER, PER)
         for i in range(PER):
             a = acc[c * PER + i]
-            o = a[:HD] / a[HD : HD + 1]
-            for side in range(2):
-                h = 2 * i + side
-                att[c, :, h * HD : (h + 1) * HD] = o[:, side * CR : (side + 1) * CR].T.astype(jnp.bfloat16)
+            o = (a[:HD] / a[HD : HD + 1]).T.astype(jnp.bfloat16)
+            for side in range(SIDE):
+                h = i * SIDE + side
+                att[c, :, h * HD : (h + 1) * HD] = o[side * CR : (side + 1) * CR]
         cps = copies(c)
         for i, (dest, half, buffer, slot) in enumerate(
             ((yo, 0, snd_a, 0), (yo, 1, snd_a, 1), (yp, 1, snd_n, 0), (ym, 0, snd_n, 1))
         ):
             buffer[c, slot] = project(c, dest, half).astype(jnp.bfloat16)
             cps[i].start()
-
-    def relay(c):
+        return carry
+
+    def relay(c, carry):
         cps = copies(c)
         for i, (dest, half) in enumerate(((yp, 0), (ym, 1))):
             part = project(c, dest, half)
             cps[i].wait_recv()
             snd_n[c, 2 + i] = (part + rcv_a[c, i].astype(jnp.float32)).astype(jnp.bfloat16)
             cps[4 + i].start()
-
-    def collect(c):
+        return carry
+
+    def collect(c, carry):
         cps = copies(c)
         own = [project(c, y, half) for half in (0, 1)]
         for i in range(2, 6):
             cps[i].wait_recv()
-        rows = slice(c * CR, (c + 1) * CR)
+        rows = pl.ds(pl.multiple_of(c * CR, CR), CR)
         out_ref[rows, :HALF] = (
             own[0] + rcv_n[c, 2].astype(jnp.float32) + rcv_n[c, 1].astype(jnp.float32)
         ).astype(jnp.bfloat16)
         out_ref[rows, HALF:] = (
             own[1] + rcv_n[c, 0].astype(jnp.float32) + rcv_n[c, 3].astype(jnp.float32)
         ).astype(jnp.bfloat16)
-
-    finish(0)
-    finish(1)
-    relay(0)
-    relay(1)
-    collect(0)
-    collect(1)
-    for c in range(CHUNKS):
-        for cp in copies(c):
+        for cp in cps:
             cp.wait_send()
+        return carry
+
+    lax.fori_loop(0, CHUNKS, finish, 0)
+    lax.fori_loop(0, CHUNKS, relay, 0)
+    lax.fori_loop(0, CHUNKS, collect, 0)
     for cp, when in pending:
         if when is None:
             cp.wait_send()
@@ -340,8 +347,8 @@
             pltpu.VMEM((CHUNKS, 1, LANES), jnp.int32),
             pltpu.VMEM((GROUPS, HD + ONES, LANES), f32),
             pltpu.VMEM((GROUPS, 1, LANES), f32),
-            pltpu.VMEM((2, 2 * TOK, LANES), f32),
-            pltpu.VMEM((2, 2 * TOK, LANES), f32),
+            pltpu.VMEM((3, 2 * TOK, LANES), f32),
+            pltpu.VMEM((3, 2 * TOK, LANES), f32),
             pltpu.VMEM((CHUNKS, CR, HEADS * HD), bf),
             pltpu.VMEM((HEADS * HD, OUT), bf),
             pltpu.VMEM((CHUNKS, 2, CR, HALF), bf),

time: 59.9 us -> 56.9 us (0.950)
  the two profiles are of different devices: /device:TPU:1 before, /device:TPU:24 now
where the time goes in v2:
time: 56.9 us; the launch traced here: 56.8 us
  Pallas kernels  54.9 us (96%)
  local copies, waits for them, and re-layouts  1.87 us (3%)
    pallas_call x1, Pallas kernels, body(): pl.pallas_call(kernel, out_shape=jax.ShapeDtypeStruct((TOK, MINE), bf), i...  54.9 us
    unnamed x1, local copies, waits for them, and re-layouts  1.87 us

profile of v2, /device:TPU:24, one launch (start us, length us, event | category | flops | bytes accessed | tf_op | source)
XLA Modules:
  0.0 56.8 jit_solution(12013242370211147783)
XLA Ops:
  0.0 54.9 %shard_map.55 = bf16[256,1024]{1,0:T(8,128)(2,1)} custom-call(bf16[256,1024]{1,0:T(8,128)(2,1)} %q_hbm.1, bf16[256,128]{1,0:T(8,128)(2,1)} %k_hbm.1, bf16[256,128]{1,0:T(8,128)(2,1)} %v_hbm.1, bf16[1024,4096]{1,0:T(8,128)(2,1)} %w_hbm.1, s32[1,256]{1,0:T(1,128)} %bitcast.1), custom_call_target="tpu_custom_call" | custom-call | flops 7000000000 | bytes 10000000 | tf_op jit(solution)/shard_map/pallas_call | solution.py:330
  54.9 1.9 %copy.7 = bf16[256,1024]{1,0:T(8,128)(2,1)} copy(bf16[256,1024]{1,0:T(8,128)(2,1)} %shard_map.55) | data formatting | bytes 1048576

commit v3 on v2

--- a/solution.py
+++ b/solution.py
@@ -31,10 +31,10 @@
 
 
 def kernel(
-    q_hbm, k_hbm, v_hbm, w_hbm, d_ref, out_ref,
-    qst, vst, qt, kb, vt, kx, vx, tk, tv, ok, ov, d2, acc, top, sa, sb, att, wv,
+    q_hbm, k_hbm, v_hbm, w_hbm, d_ref, out_hbm,
+    qst, vst, qt, kb, vt, kx, vx, tk, tv, ok, ov, d2, acc, top, sa, sb, att, wv, out,
     snd_a, rcv_a, snd_n, rcv_n,
-    lsem, wsem, gs, gr, tr, osem, ds, dr,
+    lsem, wsem, gs, gr, tr, osem, ds, dr, osems,
 ):
     ctx = lax.axis_index("ctx")
     y = lax.axis_index("tp")
@@ -161,7 +161,7 @@
             new = jnp.maximum(old, jnp.max(high, axis=0, keepdims=True))
             top[g] = new
             factor = jnp.exp2((old - new) * LOG2E_SCALE)
-            after = scores(jnp.minimum(g + 1, hi - 1), nxt, causal) if more else None
+            after = scores(g + 1, nxt, causal) if more else None
             total = None
             for j, tile in enumerate(tiles):
                 n = len(tile) * TOK
@@ -173,17 +173,15 @@
             acc[g] = acc[g] * factor + total
             return after
 
-        high = scores(lo, sa, causal)
-        if count == 2:
-            absorb(lo + 1, sb, absorb(lo, sa, high, sb), sa, more=False)
-            return
-
         def two(t, high):
             g = lo + 2 * t
             high = absorb(g, sa, high, sb)
             return absorb(g + 1, sb, high, sa)
 
-        lax.fori_loop(0, count // 2, two, high)
+        high = scores(lo, sa, causal)
+        if count > 2:
+            high = lax.fori_loop(0, count // 2 - 1, two, high)
+        absorb(hi - 1, sb, absorb(hi - 2, sa, high, sb), sa, more=False)
 
     def block(row, col, first):
         return (buf(row, col, K), buf(row, col, V), first)
@@ -198,6 +196,9 @@
         take(1, x, w)
         send((1, x), (2, x), dev_zp, w)
         sides(1, w)
+    for w in BOTH:
+        take(5, x, w)
+        send((5, x), (4, x), plane(-2), w)
     for w in BOTH:
         take(6, x, w, x < 2)
         send((6, x), (1, xo), dev_zp, w, x < 2)
@@ -208,9 +209,6 @@
         cp = pltpu.make_async_copy(w_hbm.at[pl.ds(i * 256, 256)], wv.at[pl.ds(i * 256, 256)], wsem.at[i])
         cp.start()
         wcp.append(cp)
-    for w in BOTH:
-        take(5, x, w)
-        send((5, x), (4, x), plane(-2), w)
     for w in BOTH:
         take(2, x, w)
         send((2, x), (3, x), dev_zp, w)
@@ -296,25 +294,32 @@
             cps[4 + i].start()
         return carry
 
+    def out_copy(c):
+        rows = pl.ds(pl.multiple_of(c * CR, CR), CR)
+        return pltpu.make_async_copy(out.at[rows], out_hbm.at[rows], osems.at[c])
+
     def collect(c, carry):
         cps = copies(c)
         own = [project(c, y, half) for half in (0, 1)]
         for i in range(2, 6):
             cps[i].wait_recv()
         rows = pl.ds(pl.multiple_of(c * CR, CR), CR)
-        out_ref[rows, :HALF] = (
+        out[rows, :HALF] = (
             own[0] + rcv_n[c, 2].astype(jnp.float32) + rcv_n[c, 1].astype(jnp.float32)
         ).astype(jnp.bfloat16)
-        out_ref[rows, HALF:] = (
+        out[rows, HALF:] = (
             own[1] + rcv_n[c, 0].astype(jnp.float32) + rcv_n[c, 3].astype(jnp.float32)
         ).astype(jnp.bfloat16)
         for cp in cps:
             cp.wait_send()
+        out_copy(c).start()
         return carry
 
     lax.fori_loop(0, CHUNKS, finish, 0)
     lax.fori_loop(0, CHUNKS, relay, 0)
     lax.fori_loop(0, CHUNKS, collect, 0)
+    for c in range(CHUNKS):
+        out_copy(c).wait()
     for cp, when in pending:
         if when is None:
             cp.wait_send()
@@ -331,7 +336,7 @@
         kernel,
         out_shape=jax.ShapeDtypeStruct((TOK, MINE), bf),
         in_specs=[hbm] * 4 + [vmem],
-        out_specs=vmem,
+        out_specs=hbm,
         scratch_shapes=[
             pltpu.VMEM((TOK, HEADS * HD), bf),
             pltpu.VMEM((TOK, HD), bf),
@@ -351,6 +356,7 @@
             pltpu.VMEM((3, 2 * TOK, LANES), f32),
             pltpu.VMEM((CHUNKS, CR, HEADS * HD), bf),
             pltpu.VMEM((HEADS * HD, OUT), bf),
+            pltpu.VMEM((TOK, MINE), bf),
             pltpu.VMEM((CHUNKS, 2, CR, HALF), bf),
             pltpu.VMEM((CHUNKS, 2, CR, HALF), bf),
             pltpu.VMEM((CHUNKS, 4, CR, HALF), bf),
@@ -363,6 +369,7 @@
             dma((2,)),
             dma((CHUNKS, 6)),
             dma((CHUNKS, 6)),
+            dma((CHUNKS,)),
         ],
         compiler_params=pltpu.CompilerParams(
             collective_id=0, has_side_effects=True, vmem_limit_bytes=60 << 20

time: 56.9 us -> 56 us (0.984)
  Pallas kernels: 54.9 us -> 53.8 us
    pallas_call x1, Pallas kernels: 54.9 us -> 53.8 us  [body(): pl.pallas_call(kernel, out_shape=jax.ShapeDtypeStruct((TOK, MINE), bf), i...]
where the time goes in v3:
time: 56 us; the launch traced here: 55.7 us
  Pallas kernels  53.8 us (96%)
  local copies, waits for them, and re-layouts  1.87 us (3%)
    pallas_call x1, Pallas kernels, body(): pl.pallas_call(kernel, out_shape=jax.ShapeDtypeStruct((TOK, MINE), bf), i...  53.8 us
    unnamed x1, local copies, waits for them, and re-layouts  1.87 us

profile of v3, /device:TPU:24, one launch (start us, length us, event | category | flops | bytes accessed | tf_op | source)
XLA Modules:
  0.0 55.7 jit_solution(7319769784856812118)
XLA Ops:
  0.0 53.8 %shard_map.55 = bf16[256,1024]{1,0:T(8,128)(2,1)} custom-call(bf16[256,1024]{1,0:T(8,128)(2,1)} %q_hbm.1, bf16[256,128]{1,0:T(8,128)(2,1)} %k_hbm.1, bf16[256,128]{1,0:T(8,128)(2,1)} %v_hbm.1, bf16[1024,4096]{1,0:T(8,128)(2,1)} %w_hbm.1, s32[1,256]{1,0:T(1,128)} %bitcast.1), custom_call_target="tpu_custom_call" | custom-call | flops 7000000000 | bytes 10000000 | tf_op jit(solution)/shard_map/pallas_call | solution.py:335
  53.8 1.9 %copy.7 = bf16[256,1024]{1,0:T(8,128)(2,1)} copy(bf16[256,1024]{1,0:T(8,128)(2,1)} %shard_map.55) | data formatting | bytes 1048576

commit v4 on v3

--- a/solution.py
+++ b/solution.py
@@ -229,10 +229,12 @@
     for w in BOTH:
         take(3, x, w)
         sides(3, w)
-    sweep([far(1, xo), far(2, x), far(3, x), block(4, x, (z - 4) * ROW + x * TOK)], 0, GROUPS)
+    older = [far(1, xo), far(2, x), far(3, x), block(4, x, (z - 4) * ROW + x * TOK)]
+    sweep(older, 0, GROUPS // 2)
     for w in BOTH:
         take(2, xo, w)
         send((2, xo), (3, xo), dev_zp, w)
+    sweep(older, GROUPS // 2, GROUPS // 2)
     take(2, xp)
     take(2, xm)
     take(0, xp)

time: 56 us -> 56 us (level)
  no operation moved by 1% of the time
where the time goes in v4:
time: 56 us; the launch traced here: 55.7 us
  Pallas kernels  53.8 us (96%)
  local copies, waits for them, and re-layouts  1.87 us (3%)
    pallas_call x1, Pallas kernels, body(): pl.pallas_call(kernel, out_shape=jax.ShapeDtypeStruct((TOK, MINE), bf), i...  53.8 us
    unnamed x1, local copies, waits for them, and re-layouts  1.87 us

profile of v4, /device:TPU:24, one launch (start us, length us, event | category | flops | bytes accessed | tf_op | source)
XLA Modules:
  0.0 55.7 jit_solution(3227474661733207173)
XLA Ops:
  0.0 53.8 %shard_map.55 = bf16[256,1024]{1,0:T(8,128)(2,1)} custom-call(bf16[256,1024]{1,0:T(8,128)(2,1)} %q_hbm.1, bf16[256,128]{1,0:T(8,128)(2,1)} %k_hbm.1, bf16[256,128]{1,0:T(8,128)(2,1)} %v_hbm.1, bf16[1024,4096]{1,0:T(8,128)(2,1)} %w_hbm.1, s32[1,256]{1,0:T(1,128)} %bitcast.1), custom_call_target="tpu_custom_call" | custom-call | flops 7000000000 | bytes 10000000 | tf_op jit(solution)/shard_map/pallas_call | solution.py:337
  53.8 1.9 %copy.7 = bf16[256,1024]{1,0:T(8,128)(2,1)} copy(bf16[256,1024]{1,0:T(8,128)(2,1)} %shard_map.55) | data formatting | bytes 1048576

commit v5 on v3

--- a/solution.py
+++ b/solution.py
@@ -238,6 +238,7 @@
     take(0, xp)
     take(0, xm)
     sweep([far(2, xp), far(2, xm), mixed(xp), mixed(xm)], 0, GROUPS)
+    sweep([far(2, xo)], 0, GROUPS)
     take(3, xp)
     take(3, xm)
     take(0, xo, when=x < 2)
@@ -270,7 +271,7 @@
         return jnp.dot(att[c], wv[:, cols], preferred_element_type=jnp.float32)
 
     def finish(c, carry):
-        sweep([far(2, xo), far(3, xp), far(3, xm), mixed(xo), far(3, xo)], c * PER, PER)
+        sweep([far(3, xp), far(3, xm), mixed(xo), far(3, xo)], c * PER, PER)
         for i in range(PER):
             a = acc[c * PER + i]
             o = (a[:HD] / a[HD : HD + 1]).T.astype(jnp.bfloat16)

time: 56 us -> 57.2 us (1.021)
  Pallas kernels: 53.8 us -> 55.2 us
    pallas_call x1, Pallas kernels: 53.8 us -> 55.2 us  [body(): pl.pallas_call(kernel, out_shape=jax.ShapeDtypeStruct((TOK, MINE), bf), i...]
where the time goes in v5:
time: 57.2 us; the launch traced here: 57.1 us
  Pallas kernels  55.2 us (97%)
  local copies, waits for them, and re-layouts  1.87 us (3%)
    pallas_call x1, Pallas kernels, body(): pl.pallas_call(kernel, out_shape=jax.ShapeDtypeStruct((TOK, MINE), bf), i...  55.2 us
    unnamed x1, local copies, waits for them, and re-layouts  1.87 us

profile of v5, /device:TPU:24, one launch (start us, length us, event | category | flops | bytes accessed | tf_op | source)
XLA Modules:
  0.0 57.1 jit_solution(9714498981303437744)
XLA Ops:
  0.0 55.2 %shard_map.55 = bf16[256,1024]{1,0:T(8,128)(2,1)} custom-call(bf16[256,1024]{1,0:T(8,128)(2,1)} %q_hbm.1, bf16[256,128]{1,0:T(8,128)(2,1)} %k_hbm.1, bf16[256,128]{1,0:T(8,128)(2,1)} %v_hbm.1, bf16[1024,4096]{1,0:T(8,128)(2,1)} %w_hbm.1, s32[1,256]{1,0:T(1,128)} %bitcast.1), custom_call_target="tpu_custom_call" | custom-call | flops 7000000000 | bytes 10000000 | tf_op jit(solution)/shard_map/pallas_call | solution.py:336
  55.2 1.9 %copy.7 = bf16[256,1024]{1,0:T(8,128)(2,1)} copy(bf16[256,1024]{1,0:T(8,128)(2,1)} %shard_map.55) | data formatting | bytes 1048576
